TPU v7x, 32 devices: a whole 2x2x4 slice. The times are simulated.
32 devices in a mesh: group: 2 (over x), patch: 16 (over z, y, core).
Axes of the slice: x: 2, y: 2, z: 4, core: 2. Of those that a mesh axis runs over, the one named last changes fastest.
Arguments:
- features: bfloat16 [32, 64, 4, 2304], P(('group', 'patch')), parts along dimension 0, may hold values from -6 to 6
- w_in: bfloat16 [28, 64], replicated, may hold values from -0.75 to 0.75
- w_plane: bfloat16 [9, 28, 28], replicated, may hold values from -0.375 to 0.375
- w_depth: bfloat16 [3, 28, 28], replicated, may hold values from -0.625 to 0.625
- w_head: bfloat16 [3, 28], replicated, may hold values from -1 to 1
- brick_owner: int32 [32], P(('group', 'patch')), parts along dimension 0, may hold values from 0 to 15, each once
- patch_anchor: int32 [32], P(('group', 'patch')), parts along dimension 0, may hold values from 0 to 3, as said below
- aug_code: int32 [32], P(('group', 'patch')), parts along dimension 0, may hold values from 0 to 7, as said below
Outputs:
- blended: float32 [32, 4, 2304], P(('group', 'patch')), parts along dimension 0
There are 2 independent parts, one for each index of `group`. A program takes and returns all parts, laid end to end along the dimension named above; an argument that names none is the same for every part. Nothing has to cross between parts.
Inputs may be any that keep to these rules, and one draw needn't show every extreme that they name: `brick_owner`: every device owns exactly one brick of its region. `patch_anchor`: devices 8 k to 8 k + 7 share one anchor; different positions have different anchors. `aug_code`: devices 8 k to 8 k + 7 hold each code once.
All inputs are finite; a program needn't handle non-finite values.
Results may differ from a plain program's by a relative error of at most 0.00048.
Values sent between devices are 32-bit elements; how exact they have to be, the bound alone decides.
A program may use at most 64 MiB of HBM per device.

v0:
```python
import math

import jax
import jax.numpy as jnp
from jax import lax
from jax.sharding import PartitionSpec as P


def bump_curve(length):
    position = (jnp.arange(length, dtype=jnp.float32) + 0.5) / length
    return 0.1 + jnp.sin(jnp.pi * position) ** 2


def window_volume(patch_depth, plane_side):
    return (
        bump_curve(patch_depth)[:, None, None]
        * bump_curve(plane_side)[None, :, None]
        * bump_curve(plane_side)[None, None, :]
    )


def brick_partition(volume, brick_side):
    channels, patch_depth = (volume.shape[0], volume.shape[1])
    blocks = volume.reshape(channels, patch_depth, 4, brick_side, 4, brick_side).transpose(
        2, 4, 0, 1, 3, 5
    )
    return blocks.reshape(16, channels, patch_depth * brick_side * brick_side)


def plane_shift(values, offset, plane_side):
    length = values.shape[2]
    margin = plane_side + 1
    padded = jnp.pad(values, ((0, 0), (0, 0), (margin, margin)))
    return lax.slice_in_dim(padded, margin + offset, margin + offset + length, axis=2)


def patch_output(patch_feat, flip_code, w_in, w_plane, w_depth, w_head):
    channels, patch_depth, half_plane = patch_feat.shape
    half_side = math.isqrt(half_plane)
    plane_side = 2 * half_side
    brick_side = plane_side // 4
    hidden = w_in.shape[0]
    projected = jnp.einsum(
        "oi,izp->ozp", w_in, patch_feat, preferred_element_type=jnp.float32
    ).astype(jnp.bfloat16)
    coarse_grid = projected.reshape(hidden, patch_depth, half_side, 1, half_side, 1)
    upsampled = jnp.broadcast_to(coarse_grid, (hidden, patch_depth, half_side, 2, half_side, 2))
    upsampled = upsampled.reshape(hidden, patch_depth, plane_side * plane_side)
    columns = jnp.arange(plane_side * plane_side, dtype=jnp.int32) % plane_side
    edge_masks = (
        (columns >= 1).astype(jnp.bfloat16),
        None,
        (columns <= plane_side - 2).astype(jnp.bfloat16),
    )
    mix_total = jnp.zeros((hidden, patch_depth, plane_side * plane_side), jnp.float32)
    for row_tap in range(3):
        for col_tap in range(3):
            shifted_in = plane_shift(
                upsampled, (row_tap - 1) * plane_side + col_tap - 1, plane_side
            )
            if col_tap != 1:
                shifted_in = shifted_in * edge_masks[col_tap]
            mix_total = mix_total + jnp.einsum(
                "oi,izp->ozp",
                w_plane[3 * row_tap + col_tap],
                shifted_in,
                preferred_element_type=jnp.float32,
            )
    first_out = (upsampled.astype(jnp.float32) + jax.nn.relu(mix_total)).astype(jnp.bfloat16)
    padded_depth = jnp.pad(first_out, ((0, 0), (1, 1), (0, 0)))
    mix_total = jnp.zeros((hidden, patch_depth, plane_side * plane_side), jnp.float32)
    for depth_tap in range(3):
        mix_total = mix_total + jnp.einsum(
            "oi,izp->ozp",
            w_depth[depth_tap],
            padded_depth[:, depth_tap : depth_tap + patch_depth],
            preferred_element_type=jnp.float32,
        )
    second_out = (first_out.astype(jnp.float32) + jax.nn.relu(mix_total)).astype(jnp.bfloat16)
    logits = jnp.einsum("oi,izp->ozp", w_head, second_out, preferred_element_type=jnp.float32)
    affinity = jax.nn.sigmoid(logits).reshape(3, patch_depth, plane_side, plane_side)
    affinity = jnp.where(flip_code % 2 == 1, affinity[:, ::-1], affinity)
    affinity = jnp.where(flip_code // 2 % 2 == 1, affinity[:, :, ::-1], affinity)
    affinity = jnp.where(flip_code // 4 % 2 == 1, affinity[:, :, :, ::-1], affinity)
    window = window_volume(patch_depth, plane_side)
    weighted = affinity * window[None]
    weighted = jnp.concatenate([weighted, window[None]], axis=0)
    return (brick_partition(weighted, brick_side), window)


def on_device(features, w_in, w_plane, w_depth, w_head, brick_owner, patch_anchor, aug_code):
    devices = lax.axis_size("patch")
    brick_rows = devices // 4
    owner_lookup = lax.all_gather(brick_owner, "patch", axis=0, tiled=True)
    volume_bricks, window = patch_output(features[0], aug_code[0], w_in, w_plane, w_depth, w_head)
    tile_index = jnp.arange(16, dtype=jnp.int32)
    device_ids = jnp.arange(devices, dtype=jnp.int32)
    brick_id = (patch_anchor[0] + tile_index // 4) % brick_rows * 4 + tile_index % 4
    table_hits = brick_id[:, None] == device_ids[None, :]
    owners = jnp.sum(jnp.where(table_hits, owner_lookup[None, :], 0), axis=1)
    delivery_routes = (owners[None, :] == device_ids[:, None]).astype(jnp.float32)
    departing_pieces = jnp.einsum(
        "ve,eig->vig", delivery_routes, volume_bricks, precision=lax.Precision.HIGHEST
    )
    received = lax.all_to_all(departing_pieces, "patch", split_axis=0, concat_axis=0, tiled=True)
    arrived = jnp.sum(received, axis=0, keepdims=True)
    return arrived


def solution(mesh):
    in_specs = (
        P(("group", "patch"), None, None, None),
        P(),
        P(),
        P(),
        P(),
        P(("group", "patch")),
        P(("group", "patch")),
        P(("group", "patch")),
    )
    out_specs = P(("group", "patch"), None, None)
    return jax.shard_map(
        on_device, mesh=mesh, in_specs=in_specs, out_specs=out_specs, check_vma=False
    )
```

profile of v0, /device:TPU:0, one launch (start us, length us, event | category | flops | bytes accessed | tf_op | source)
XLA Modules:
  0.0 95.0 jit_solution(16755403858895298420)
XLA Ops:
  0.0 0.6 fusion.46
  0.6 0.6 fusion.47
  2.1 0.1 multiply_add_fusion
  2.2 1.8 %convolution_convert_fusion = bf16[28,4,2304]{2,0,1:T(8,128)(2,1)} fusion(bf16[64,4,2304]{2,1,0:T(4,128)(2,1)S(1)} %bitcast.99, bf16[28,64]{1,0:T(8,128)(2,1)} %param.9), kind=kOutput, calls=%fused_computation.23 | convolution fusion | flops 33288192 | bytes 1699328 | tf_op jit(solution)/shard_map/oi,izp->ozp/dot_general | solution.py:43
  4.0 2.1 %copy.40 = bf16[28,4,2304]{0,2,1:T(8,128)(2,1)S(1)} copy(bf16[28,4,2304]{2,0,1:T(8,128)(2,1)} %convolution_convert_fusion) | data formatting | bytes 1032192 | tf_op jit(solution)/shard_map/broadcast_in_dim | solution.py:47
  6.0 7.1 %broadcast_in_dim.17 = bf16[28,4,48,2,48,2]{0,5,4,3,2,1:T(2,128)(2,1)} broadcast(bf16[28,4,48,48]{0,3,2,1:T(8,128)(2,1)S(1)} %bitcast.104), dimensions={0,1,2,4} | broadcast | bytes 2580480 | tf_op jit(solution)/shard_map/broadcast_in_dim | solution.py:47
  13.1 7.5 %copy.31 = bf16[28,4,9216]{2,0,1:T(8,128)(2,1)S(1)} copy(bf16[28,4,9216]{0,2,1:T(8,128)(2,1)} %bitcast.100) | data formatting | bytes 4128768 | tf_op jit(solution)/shard_map/reshape | solution.py:48
  20.7 1.1 %fusion.24 = f32[4,9216,28]{1,2,0:T(8,128)S(1)} fusion(bf16[9216]{0:T(1024)(128)(2,1)S(1)} %copy-done.3, bf16[28,4,9216]{2,0,1:T(8,128)(2,1)S(1)} %copy.31, bf16[9,28,28]{2,1,0:T(8,128)(2,1)S(1)} %copy-done.5), kind=kOutput, calls=%fused_computation.37 | convolution fusion | flops 61931520 | bytes 6514688 | tf_op jit(solution)/shard_map/oi,izp->ozp/dot_general | solution.py:63
  21.8 1.3 %convolution_add_fusion.9 = f32[4,9216,28]{1,2,0:T(8,128)S(1)} fusion(f32[4,9216,28]{1,2,0:T(8,128)S(1)} %fusion.24, bf16[28,4,9216]{2,0,1:T(8,128)(2,1)S(1)} %copy.31, bf16[9,28,28]{2,1,0:T(8,128)(2,1)S(1)} %copy-done.5), kind=kOutput, calls=%fused_computation.15 | convolution fusion | flops 58834944 | bytes 11214848 | tf_op jit(solution)/shard_map/oi,izp->ozp/dot_general | solution.py:63
  23.1 0.0 slice-start
  23.2 1.4 %convolution_add_fusion.8 = f32[4,9216,28]{1,2,0:T(8,128)S(1)} fusion(f32[4,9216,28]{1,2,0:T(8,128)S(1)} %convolution_add_fusion.9, bf16[9216]{0:T(1024)(128)(2,1)S(1)} %copy-done.4, bf16[28,4,9216]{2,0,1:T(8,128)(2,1)S(1)} %copy.31, bf16[9,28,28]{2,1,0:T(8,128)(2,1)S(1)} %copy-done.5), kind=kOutput, calls=%fused_computation.14 | convolution fusion | flops 62963712 | bytes 11233280 | tf_op jit(solution)/shard_map/oi,izp->ozp/dot_general | solution.py:63
  24.6 0.0 slice-start.2
  24.6 1.4 %convolution_add_fusion.7 = f32[4,9216,28]{1,2,0:T(8,128)S(1)} fusion(f32[4,9216,28]{1,2,0:T(8,128)S(1)} %convolution_add_fusion.8, bf16[9216]{0:T(1024)(128)(2,1)S(1)} %copy-done.3, bf16[28,4,9216]{2,0,1:T(8,128)(2,1)S(1)} %copy.31, bf16[9,28,28]{2,1,0:T(8,128)(2,1)S(1)} %copy-done.5), kind=kOutput, calls=%fused_computation.13 | convolution fusion | flops 62963712 | bytes 11233280 | tf_op jit(solution)/shard_map/oi,izp->ozp/dot_general | solution.py:63
  26.0 0.6 slice-done.1
  26.6 0.4 slice-done.2
  27.0 3.4 %convolution_add_fusion.6 = f32[4,9216,28]{1,2,0:T(8,128)S(1)} fusion(f32[4,9216,28]{1,2,0:T(8,128)S(1)} %convolution_add_fusion.7, bf16[28,4,9216]{0,2,1:T(8,128)(2,1)S(1)} %bitcast.103, bf16[9,28,28]{2,1,0:T(8,128)(2,1)S(1)} %copy-done.5), kind=kOutput, calls=%fused_computation.12 | convolution fusion | flops 58834944 | bytes 18292736 | tf_op jit(solution)/shard_map/oi,izp->ozp/dot_general | solution.py:63
  30.4 1.4 %convolution_add_fusion.5 = f32[4,9216,28]{1,2,0:T(8,128)S(1)} fusion(f32[4,9216,28]{1,2,0:T(8,128)S(1)} %convolution_add_fusion.6, bf16[9216]{0:T(1024)(128)(2,1)S(1)} %copy-done.4, bf16[28,4,9216]{2,0,1:T(8,128)(2,1)S(1)} %copy.31, bf16[9,28,28]{2,1,0:T(8,128)(2,1)S(1)} %copy-done.5), kind=kOutput, calls=%fused_computation.11 | convolution fusion | flops 62963712 | bytes 11233280 | tf_op jit(solution)/shard_map/oi,izp->ozp/dot_general | solution.py:63
  31.8 1.4 %convolution_add_fusion.4 = f32[4,9216,28]{1,2,0:T(8,128)S(1)} fusion(f32[4,9216,28]{1,2,0:T(8,128)S(1)} %convolution_add_fusion.5, bf16[9216]{0:T(1024)(128)(2,1)S(1)} %copy-done.3, bf16[28,4,9216]{2,0,1:T(8,128)(2,1)S(1)} %copy.31, bf16[9,28,28]{2,1,0:T(8,128)(2,1)S(1)} %copy-done.5), kind=kOutput, calls=%fused_computation.10 | convolution fusion | flops 62963712 | bytes 11233280 | tf_op jit(solution)/shard_map/oi,izp->ozp/dot_general | solution.py:63
  33.2 1.3 %convolution_add_fusion.3 = f32[4,9216,28]{1,2,0:T(8,128)S(1)} fusion(f32[4,9216,28]{1,2,0:T(8,128)S(1)} %convolution_add_fusion.4, bf16[28,4,9216]{2,0,1:T(8,128)(2,1)S(1)} %copy.31, bf16[9,28,28]{2,1,0:T(8,128)(2,1)S(1)} %copy-done.5), kind=kOutput, calls=%fused_computation.9 | convolution fusion | flops 58834944 | bytes 11214848 | tf_op jit(solution)/shard_map/oi,izp->ozp/dot_general | solution.py:63
  34.5 0.0 copy-start.6
  34.5 1.9 %fusion.6 = bf16[28,4,9216]{2,0,1:T(8,128)(2,1)S(1)} fusion(f32[4,9216,28]{1,2,0:T(8,128)S(1)} %convolution_add_fusion.3, bf16[28,4,9216]{2,0,1:T(8,128)(2,1)S(1)} %copy.31, bf16[9216]{0:T(1024)(128)(2,1)S(1)} %copy-done.4, bf16[9,28,28]{2,1,0:T(8,128)(2,1)S(1)} %copy-done.5), kind=kOutput, calls=%fused_computation.16 | convolution fusion | flops 67092480 | bytes 11528192 | tf_op jit(solution)/shard_map/oi,izp->ozp/dot_general | solution.py:63
  36.4 1.0 %fusion.51 = f32[4,9216,28]{1,2,0:T(8,128)S(1)} fusion(bf16[28,4,9216]{2,0,1:T(8,128)(2,1)S(1)} %fusion.6, bf16[3,28,28]{2,1,0:T(8,128)(2,1)S(1)} %copy-done.6), kind=kOutput, calls=%fused_computation.70 | convolution fusion | flops 57802752 | bytes 6496256 | tf_op jit(solution)/shard_map/oi,izp->ozp/dot_general | solution.py:73
  37.4 0.5 copy-done.2
  37.9 3.1 %convolution_add_fusion.1 = f32[4,9216,28]{1,2,0:T(8,128)} fusion(f32[4,9216,28]{1,2,0:T(8,128)S(1)} %fusion.51, bf16[28,4,9216]{2,0,1:T(8,128)(2,1)S(1)} %fusion.6, bf16[3,28,28]{2,1,0:T(8,128)(2,1)S(1)} %copy-done.6), kind=kOutput, calls=%fused_computation.4 | convolution fusion | flops 44384256 | bytes 11214848 | tf_op jit(solution)/shard_map/oi,izp->ozp/dot_general | solution.py:73
  40.9 4.8 %fusion.11 = f32[3,4,9216]{2,0,1:T(4,128)S(1)} fusion(f32[4,9216,28]{1,2,0:T(8,128)} %convolution_add_fusion.1, bf16[28,4,9216]{2,0,1:T(8,128)(2,1)} %copy-done.2, bf16[3,28,28]{2,1,0:T(8,128)(2,1)S(1)} %copy-done.6, bf16[3,28]{1,0:T(4,128)(2,1)S(1)} %copy-done.7), kind=kOutput, calls=%fused_computation.22 | convolution fusion | flops 55037952 | bytes 9888768 | tf_op jit(solution)/shard_map/oi,izp->ozp/dot_general | solution.py:80
  45.7 0.3 copy.34
  46.0 0.3 reshape.138
  46.4 0.3 rev.10
  46.8 0.1 broadcast_select_fusion
  46.9 1.0 %rev.11 = f32[3,4,96,96]{3,2,1,0:T(8,128)S(1)} reverse(f32[3,4,96,96]{3,2,1,0:T(8,128)S(1)} %broadcast_select_fusion), dimensions={3} | reverse | bytes 884736 | tf_op jit(solution)/shard_map/rev | solution.py:84
  47.9 0.1 broadcast_multiply_fusion.3
  47.9 0.1 broadcast_multiply_fusion.1
  48.1 0.9 select_multiply_fusion
  49.0 2.2 %concatenate.6 = f32[3,4,4,24,4,24]{5,4,3,2,1,0:T(4,128)S(1)} reshape(f32[3,4,96,96]{3,2,1,0:T(8,128)} %select_multiply_fusion) | data formatting | bytes 884736 | tf_op jit(solution)/shard_map/concatenate | solution.py:87
  51.2 0.3 copy.35
  51.5 0.1 broadcast_multiply_fusion.2
  51.5 0.2 broadcast_multiply_fusion
  52.4 0.0 copy-start.8
  52.4 1.9 %maximum_bitcast_fusion = f32[4,4,4,4,24,24]{5,4,3,1,0,2:T(8,128)} fusion(f32[1,4,4,24,4,24]{5,3,1,4,2,0:T(8,128)S(1)} %broadcast_multiply_fusion, f32[3,4,4,24,4,24]{5,3,1,4,2,0:T(8,128)S(1)} %copy.35), kind=kLoop, calls=%fused_computation.24 | loop fusion | flops 147456 | bytes 1179648 | tf_op jit(solution)/shard_map/transpose | solution.py:24
  54.3 0.6 dynamic-slice
  54.9 0.9 dynamic-update-slice
  55.8 3.3 %reshape.139 = f32[16,4,2304]{2,0,1:T(8,128)S(1)} reshape(f32[4,4,4,4,24,24]{5,4,3,1,0,2:T(8,128)} %maximum_bitcast_fusion) | data formatting | bytes 1179648 | tf_op jit(solution)/shard_map/reshape | solution.py:27
  59.0 13.7 %all-reduce.2 = s32[16]{0:T(128)S(1)} all-reduce(s32[16]{0:T(128)S(1)} %dynamic-update-slice), channel_id=1, replica_groups=mesh['group'=2,'patch'=16] {'patch'}, use_global_device_ids=true, to_apply=%add.2 | all-reduce | flops 16 | bytes 128
  73.5 0.2 select_reduce_fusion
  73.6 0.4 fusion.78
  74.0 0.4 copy.36
  74.4 19.8 %all_to_all.5 = f32[16,4,2304]{2,1,0:T(4,128)S(1)} all-to-all(f32[16,4,2304]{2,1,0:T(4,128)S(1)} %copy.36), channel_id=1, replica_groups=mesh['group'=2,'patch'=16] {'patch'}, dimensions={0} | all-to-all | bytes 1179648 | tf_op jit(solution)/shard_map/all_to_all | solution.py:105
  94.3 0.7 reduce_sum.19
  (23 shorter events, 0.2 us)
Async XLA Ops:
  0.0 2.1 %copy-start = (bf16[1,64,4,2304]{3,2,1,0:T(4,128)(2,1)S(1)}, bf16[1,64,4,2304]{3,2,1,0:T(4,128)(2,1)}, u32[]{:S(2)}) copy-start(bf16[1,64,4,2304]{3,2,1,0:T(4,128)(2,1)} %param.8) | copy-start | bytes 3538948
  13.1 7.6 %copy-start.3 = (bf16[9216]{0:T(1024)(128)(2,1)S(1)}, bf16[9216]{0:T(1024)(128)(2,1)}, u32[]{:S(2)}) copy-start(bf16[9216]{0:T(1024)(128)(2,1)} %fusion.46) | copy-start | bytes 55300
  13.1 7.6 %copy-start.5 = (bf16[9,28,28]{2,1,0:T(8,128)(2,1)S(1)}, bf16[9,28,28]{2,1,0:T(8,128)(2,1)}, u32[]{:S(2)}) copy-start(bf16[9,28,28]{2,1,0:T(8,128)(2,1)} %param.10) | copy-start | bytes 42340
  21.8 1.3 %copy-start.4 = (bf16[9216]{0:T(1024)(128)(2,1)S(1)}, bf16[9216]{0:T(1024)(128)(2,1)}, u32[]{:S(2)}) copy-start(bf16[9216]{0:T(1024)(128)(2,1)} %fusion.47) | copy-start | bytes 55300
  23.1 2.9 %slice-start = ((s8[9437184]{0:T(1024)(128)(4,1)}), s8[4194304]{0:T(1024)(128)(4,1)S(1)}, s32[]{:S(2)}) async-start(s8[9437184]{0:T(1024)(128)(4,1)} %bitcast.101), calls=%async_computation.1 | async-start | bytes 8388608
  23.1 3.5 %slice-start.1 = ((s8[9437184]{0:T(1024)(128)(4,1)}), s8[4194304]{0:T(1024)(128)(4,1)S(1)}, s32[]{:S(2)}) async-start(s8[9437184]{0:T(1024)(128)(4,1)} %bitcast.101), calls=%async_computation.2 | async-start | bytes 8388608
  24.6 2.5 %slice-start.2 = ((s8[9437184]{0:T(1024)(128)(4,1)}), s8[1048576]{0:T(1024)(128)(4,1)S(1)}, s32[]{:S(2)}) async-start(s8[9437184]{0:T(1024)(128)(4,1)} %bitcast.101), calls=%async_computation.3 | async-start | bytes 2097152
  34.5 1.9 %copy-start.6 = (bf16[3,28,28]{2,1,0:T(8,128)(2,1)S(1)}, bf16[3,28,28]{2,1,0:T(8,128)(2,1)}, u32[]{:S(2)}) copy-start(bf16[3,28,28]{2,1,0:T(8,128)(2,1)} %param.11) | copy-start | bytes 14116
  36.4 1.4 %copy-start.2 = (bf16[28,4,9216]{2,0,1:T(8,128)(2,1)}, bf16[28,4,9216]{2,0,1:T(8,128)(2,1)S(1)}, u32[]{:S(2)}) copy-start(bf16[28,4,9216]{2,0,1:T(8,128)(2,1)S(1)} %fusion.6) | copy-start | bytes 6193156
  37.9 3.1 %copy-start.7 = (bf16[3,28]{1,0:T(4,128)(2,1)S(1)}, bf16[3,28]{1,0:T(4,128)(2,1)}, u32[]{:S(2)}) copy-start(bf16[3,28]{1,0:T(4,128)(2,1)} %param.12) | copy-start | bytes 508
  52.4 2.0 %copy-start.8 = (u32[32]{0:T(128)S(1)}, u32[32]{0:T(128)}, u32[]{:S(2)}) copy-start(u32[32]{0:T(128)} %constant.126) | copy-start | bytes 388
  54.9 40.1 %copy-start.1 = (bf16[1,64,4,2304]{3,2,1,0:T(4,128)(2,1)S(1)}, bf16[1,64,4,2304]{3,2,1,0:T(4,128)(2,1)}, u32[]{:S(2)}) copy-start(bf16[1,64,4,2304]{3,2,1,0:T(4,128)(2,1)} %param.8) | copy-start | bytes 3538948
where the time goes:
time: 95.4 us; the launch traced here: 95 us
  blocking collectives  33.6 us (35%)
  local copies, waits for them, and re-layouts  27.7 us (29%)
  matrix products  25.6 us (27%)
  other arithmetic  5.69 us (6%)
  between operations  2.36 us (2%)
    all_to_all x1, blocking collectives, on_device(): lax.all_to_all(departing_pieces, 'patch', split_axis=0, concat_axis=0, ti...  19.8 us
    dot_general x9, matrix products, patch_output(): jnp.einsum('oi,izp->ozp', w_plane[3 * row_tap + col_tap], shifted_in, pre...  14.6 us
    unnamed x1, blocking collectives  13.7 us
    broadcast_in_dim x2, local copies, waits for them, and re-layouts, patch_output(): jnp.broadcast_to(coarse_grid, (hidden, patch_depth, half_side, 2, half_si...  9.15 us
    reshape x1, local copies, waits for them, and re-layouts, patch_output(): upsampled = upsampled.reshape(hidden, patch_depth, plane_side * plane_side)  7.54 us
    dot_general x1, matrix products, patch_output(): jnp.einsum('oi,izp->ozp', w_head, second_out, preferred_element_type=jnp....  4.8 us
    dot_general x2, matrix products, patch_output(): jnp.einsum('oi,izp->ozp', w_depth[depth_tap], padded_depth[:, depth_tap:d...  4.02 us
    reshape x1, local copies, waits for them, and re-layouts, brick_partition(): return blocks.reshape(16, channels, patch_depth * brick_side * brick_side)  3.29 us

commit v1 on v0

v1 whole, which is shorter than its diff:
```python
import functools
import math

import jax
import jax.numpy as jnp
import numpy as np
from jax import lax
from jax.experimental import pallas as pl
from jax.experimental.pallas import tpu as pltpu
from jax.sharding import PartitionSpec as P

MESH = pl.DeviceIdType.MESH
LANES = 128
PAD = 32
F32 = jnp.float32
BF16 = jnp.bfloat16


def bump(length):
    position = (np.arange(length) + 0.5) / length
    return 0.1 + np.sin(np.pi * position) ** 2


def tables(half, depth):
    hb = half // 4
    cells = hb * hb
    rest = cells - LANES
    block = hb * half
    side = 2 * half
    fine = 4 * cells
    yc, xc = np.divmod(np.arange(cells), hb)
    groups = LANES // rest
    place = np.zeros((4, block, 8 * LANES), np.float32)
    for flip in range(4):
        fy, fx = flip % 2, flip // 2
        for j in range(4):
            ys = hb - 1 - yc if fy else yc
            xs = half - 1 - (hb * j + xc) if fx else hb * j + xc
            lane = ys * half + xs
            m = np.arange(LANES)
            place[flip, lane[:LANES], j * LANES + m] = 1
            for g in range(groups):
                place[flip, lane[LANES:], (4 + j) * LANES + rest * g + np.arange(rest)] = 1
    spread = np.zeros((2, 4 * LANES, fine), np.float32)
    for py in range(2):
        for px in range(2):
            cell = (2 * yc + py) * (2 * hb) + 2 * xc + px
            spread[py, px * LANES + np.arange(LANES), cell[:LANES]] = 1
            for g in range(groups):
                spread[py, (2 + px) * LANES + rest * g + np.arange(rest), cell[LANES:]] = 1
    bz, by = bump(depth), bump(side)
    win = np.zeros((16, 24, LANES), np.float32)
    win_out = np.zeros((16, 1, depth * fine), np.float32)
    for i in range(4):
        for j in range(4):
            rows = by[2 * hb * i : 2 * hb * (i + 1)]
            cols = by[2 * hb * j : 2 * hb * (j + 1)]
            win_out[i * 4 + j, 0] = (bz[:, None, None] * rows[None, :, None] * cols[None, None, :]).reshape(-1)
            for py in range(2):
                for px in range(2):
                    value = bz[:, None] * (rows[2 * yc + py] * cols[2 * xc + px])[None]
                    win[i * 4 + j, 8 * py + px * 4 : 8 * py + px * 4 + 4] = value[:, :LANES]
                    for k in range(3):
                        at = rest * (3 * py + k)
                        win[i * 4 + j, 16 + px * 4 : 20 + px * 4, at : at + rest] = value[:, LANES:]
    return (
        jnp.asarray(place, BF16),
        jnp.asarray(spread, BF16),
        jnp.asarray(win, F32),
        jnp.asarray(win_out, F32),
    )


def shifted(values, offset):
    rows, length = values.shape
    zeros = jnp.zeros((rows, abs(offset)), values.dtype)
    if offset > 0:
        return jnp.concatenate([values[:, offset:], zeros], axis=1)
    return jnp.concatenate([zeros, values[:, : length + offset]], axis=1)


def dot(a, b):
    return jnp.dot(a, b, preferred_element_type=F32)


def split(values):
    high = values.astype(BF16)
    return high, (values - high.astype(F32)).astype(BF16)


def kernel(
    n, half,
    feat, w_in, w_plane, w_depth, w_head, owner_s, anchor_s, code_s, place_h, spread_h, win_h, win_out_h,
    out,
    place, spread, win, win_out, table_sem,
    wi_s, wp_s, wd_s, wh_s, xs, first_s, second_s, br0, br1,
    say, heard, inverse_v, inverse_s, inverse_sem, say_sem, hear_sem,
    pair_out0, pair_in0, kept0, cross_out0, cross_in0,
    pair_out1, pair_in1, kept1, cross_out1, cross_in1,
    pair_send, pair_recv, cross_send, cross_recv,
):
    hidden = w_in.shape[0]
    cin = w_in.shape[1]
    depth = feat.shape[2]
    plane = half * half
    block = plane // 4
    chips = n // 2
    brick_rows = n // 4
    rest = plane // 16 - LANES
    fine = plane // 4
    me = lax.axis_index("patch")
    chip, core = me // 2, lax.rem(me, 2)
    partner = me + 1 - 2 * core

    loads = [
        pltpu.make_async_copy(h, v, table_sem.at[s])
        for s, (h, v) in enumerate(((place_h, place), (win_h, win), (spread_h, spread), (win_out_h, win_out)))
    ]
    for load in loads:
        load.start()

    barrier = pltpu.get_barrier_semaphore()
    for off in range(1, n):
        pl.semaphore_signal(barrier, inc=1, device_id={"patch": lax.rem(me + off, n)}, device_id_type=MESH)

    code = code_s[0]
    anchor = anchor_s[0]
    fz, fy, fx = code % 2, (code // 2) % 2, code // 4
    word = jnp.concatenate(
        [jnp.full((1, LANES), owner_s[0], jnp.int32), jnp.full((1, LANES), anchor, jnp.int32)], axis=0
    )
    say[...] = word
    heard[me] = word

    spread_cols = lax.broadcasted_iota(jnp.int32, (cin, cin * depth), 1) // depth
    spread_rows = lax.broadcasted_iota(jnp.int32, (cin, cin * depth), 0)
    wi_all = dot(w_in[...], (spread_cols == spread_rows).astype(F32).astype(BF16))
    section = lax.broadcasted_iota(jnp.int32, (hidden, cin * depth), 1) % depth
    wi_s[...] = jnp.zeros_like(wi_s)
    for z in range(depth):
        wi_s[PAD * z : PAD * z + hidden, :] = jnp.where(section == z, wi_all, 0.0)
    wp_s[...] = jnp.zeros_like(wp_s)
    taps = [w_plane[t].astype(F32) for t in range(9)]
    halves = (((0,), (1, 2)), ((0, 1), (2,)))
    for sy in range(2):
        for dyi in range(2):
            for px in range(2):
                for at, txs in enumerate(halves[px]):
                    total = sum(taps[3 * ty + tx] for ty in halves[sy][dyi] for tx in txs)
                    col = PAD * (3 * dyi + px + at)
                    wp_s[sy, PAD * px : PAD * px + hidden, col : col + hidden] = total
    wd_s[...] = jnp.zeros_like(wd_s)
    for z in range(depth):
        for tz in range(3):
            if 0 <= z + tz - 1 < depth:
                col = PAD * (z + tz - 1)
                wd_s[PAD * z : PAD * z + hidden, col : col + hidden] = w_depth[tz].astype(F32)
    wh_s[...] = jnp.zeros_like(wh_s)
    for m in range(2 * depth):
        wh_s[:, PAD * m : PAD * m + hidden] = w_head[...].astype(F32)
    row8 = lax.broadcasted_iota(jnp.int32, (8, 2 * depth * PAD), 0)
    col8 = lax.broadcasted_iota(jnp.int32, (8, 2 * depth * PAD), 1) // PAD
    z_from = jnp.where(fz == 1, depth - 1 - col8 % depth, col8 % depth)
    px_from = jnp.where(fx == 1, 1 - col8 // depth, col8 // depth)
    wanted = row8 == px_from * depth + z_from
    head = jnp.concatenate(
        [jnp.where(wanted, jnp.broadcast_to(wh_s[k : k + 1, :], wanted.shape), 0.0) for k in range(3)], axis=0
    ).astype(BF16)
    depth_w = wd_s[...].astype(BF16)

    x = dot(wi_s[...].astype(BF16), feat[0].reshape(cin * depth, plane)).astype(BF16)
    lane_x = lax.broadcasted_iota(jnp.int32, (1, plane), 1) % half
    left = shifted(x, -1) * (lane_x >= 1).astype(F32).astype(BF16)
    right = shifted(x, 1) * (lane_x <= half - 2).astype(F32).astype(BF16)
    for dx, values in enumerate((left, x, right)):
        xs[0, dx] = shifted(values, -half)
        xs[1, dx] = values
        xs[2, dx] = shifted(values, half)

    pl.semaphore_wait(barrier, n - 1)
    tells = []
    for off in range(1, n):
        tells.append(
            pltpu.make_async_remote_copy(
                src_ref=say, dst_ref=heard.at[me], send_sem=say_sem.at[off - 1], recv_sem=hear_sem.at[off - 1],
                device_id={"patch": lax.rem(me + off, n)}, device_id_type=MESH,
            )
        )
        tells[-1].start()

    lane = lax.broadcasted_iota(jnp.int32, (8, LANES), 1) // rest

    def planes(qy):
        sy = jnp.where(fy == 1, 1 - qy, qy)
        w_high, w_low = split(wp_s[sy])
        weights = jnp.concatenate([w_high, w_low], axis=0)
        around = [xs[sy + dyi, dx] for dyi in range(2) for dx in range(3)]
        for z in range(depth):
            rows = slice(PAD * z, PAD * (z + 1))
            mixed = dot(weights, jnp.concatenate([a[rows] for a in around], axis=0))
            mixed = mixed[: 2 * PAD] + mixed[2 * PAD :]
            up = xs[1, 1, rows, :].astype(F32)
            for px in range(2):
                first = up + jnp.maximum(mixed[PAD * px : PAD * (px + 1)], 0.0)
                first_s[px, rows, :] = first.astype(BF16)

    def heads(qy, brick):
        for px in range(2):
            first = first_s[px]
            second = first.astype(F32) + jnp.maximum(dot(depth_w, first), 0.0)
            second_s[depth * PAD * px : depth * PAD * (px + 1), :] = second.astype(BF16)
        affinity = jax.nn.sigmoid(dot(head, second_s[...]))
        both = jnp.concatenate(split(affinity), axis=0)
        stacked = jnp.concatenate([both[:, block * i : block * (i + 1)] for i in range(4)], axis=0)
        if qy == 0:
            loads[0].wait()
        placed = dot(stacked, place[code // 2])
        for i in range(4):
            value = placed[48 * i : 48 * i + 24] + placed[48 * i + 24 : 48 * i + 48]
            for j in range(4):
                e = 4 * i + j
                brick[e, 0:24, :] = value[:, LANES * j : LANES * (j + 1)]
                tail = value[:, LANES * (4 + j) : LANES * (5 + j)]
                tail = sum(jnp.where(lane == 3 * qy + k, tail[8 * k : 8 * k + 8], 0.0) for k in range(3))
                if qy == 0:
                    br1[e, 24:32, :] = tail
                else:
                    br1[e, 24:32, :] = br1[e, 24:32, :] + tail

    def piece(qy, brick, v):
        b = inverse_s[0, v]
        i = lax.rem(b // 4 - anchor + brick_rows, brick_rows)
        valid = (i < 4).astype(F32)
        i = jnp.minimum(i, 3)
        j = lax.rem(b, 4)
        source = jnp.where(fy == 1, 3 - i, i)
        window = win[4 * i + j]
        part = window[8 * qy : 8 * qy + 8]
        window = jnp.concatenate([part] * 3 + ([window[16:24]] if qy else []), axis=0)
        return brick[4 * source + j] * window * valid

    def pair_start(qy, brick, pair_out, pair_in, kept):
        for t in range(chips):
            pair_out[t] = piece(qy, brick, 2 * t + 1 - core)
        copy = pltpu.make_async_remote_copy(
            src_ref=pair_out, dst_ref=pair_in, send_sem=pair_send.at[qy], recv_sem=pair_recv.at[qy],
            device_id={"patch": partner}, device_id_type=MESH,
        )
        copy.start()
        for t in range(chips):
            kept[t] = piece(qy, brick, 2 * t + core)
        return copy

    def cross_start(qy, copy, pair_in, kept, cross_out, cross_in):
        copy.wait()
        copies = []
        for off in range(1, chips):
            t = lax.rem(chip + off, chips)
            cross_out[off - 1] = kept[t] + pair_in[t]
            copies.append(
                pltpu.make_async_remote_copy(
                    src_ref=cross_out.at[off - 1], dst_ref=cross_in.at[off - 1],
                    send_sem=cross_send.at[qy, off - 1], recv_sem=cross_recv.at[qy, off - 1],
                    device_id={"patch": 2 * t + core}, device_id_type=MESH,
                )
            )
            copies[-1].start()
        return copies

    def cross_end(copies, pair_in, kept, cross_in):
        total = kept[chip] + pair_in[chip]
        for at, copy in enumerate(copies):
            copy.wait()
            total = total + cross_in[at]
        return total

    planes(0)
    for tell in tells:
        tell.wait()
    lane1 = lax.broadcasted_iota(jnp.int32, (1, LANES), 1)
    inverse_v[...] = sum(jnp.where(heard[d, 0:1, :] == lane1, d, 0) for d in range(n))
    fetch = pltpu.make_async_copy(inverse_v, inverse_s, inverse_sem)
    fetch.start()
    heads(0, br0)
    fetch.wait()
    loads[1].wait()
    pair0 = pair_start(0, br0, pair_out0, pair_in0, kept0)
    planes(1)
    cross0 = cross_start(0, pair0, pair_in0, kept0, cross_out0, cross_in0)
    heads(1, br1)
    pair1 = pair_start(1, br1, pair_out1, pair_in1, kept1)
    cross1 = cross_start(1, pair1, pair_in1, kept1, cross_out1, cross_in1)

    loads[2].wait()
    loads[3].wait()
    mine = inverse_s[0, me]
    window = jnp.zeros((1, win_out.shape[2]), F32)
    for i in range(4):
        count = jnp.zeros((1, LANES), F32)
        for d in range(n):
            at = mine // 4 - heard[d, 1:2, :]
            at = jnp.where(at < 0, at + brick_rows, at)
            count = count + jnp.where(at == i, 1.0, 0.0)
        window = window + count[:, 0:1] * win_out[4 * i + lax.rem(mine, 4)]
    out[0, 3:4, :] = window

    totals = (
        cross_end(cross0, pair_in0, kept0, cross_in0),
        cross_end(cross1, pair_in1, kept1, cross_in1),
    )
    tail = totals[1][24:32]
    right_px = lax.broadcasted_iota(jnp.int32, (24, LANES), 0) // 4 % 2 == 1
    result = jnp.zeros((24, fine), F32)
    for py in range(2):
        main = totals[py][0:24]
        tails = jnp.concatenate([jnp.where(lane == 3 * py + k, tail, 0.0) for k in range(3)], axis=0)
        wide = jnp.concatenate(
            [
                jnp.where(right_px, 0.0, main), jnp.where(right_px, main, 0.0),
                jnp.where(right_px, 0.0, tails), jnp.where(right_px, tails, 0.0),
            ],
            axis=1,
        )
        both = dot(jnp.concatenate(split(wide), axis=0), spread[py])
        result = result + (both[:24] + both[24:])
    for k in range(3):
        for z in range(depth):
            row = 8 * k + z
            out[0, k : k + 1, fine * z : fine * (z + 1)] = result[row : row + 1] + result[row + 4 : row + 5]


def on_device(features, w_in, w_plane, w_depth, w_head, brick_owner, patch_anchor, aug_code):
    n = lax.axis_size("patch")
    _, cin, depth, plane = features.shape
    half = math.isqrt(plane)
    block = plane // 4
    chips = n // 2
    place, spread, win, win_out = tables(half, depth)
    vmem = pl.BlockSpec(memory_space=pltpu.VMEM)
    smem = pl.BlockSpec(memory_space=pltpu.SMEM)
    hbm = pl.BlockSpec(memory_space=pl.ANY)
    rows = depth * PAD
    V = pltpu.VMEM
    dma = pltpu.SemaphoreType.DMA
    exchange = []
    for height in (24, 32):
        exchange += [V((chips, height, LANES), F32)] * 3 + [V((chips - 1, height, LANES), F32)] * 2
    return pl.pallas_call(
        functools.partial(kernel, n, half),
        out_shape=jax.ShapeDtypeStruct((1, 4, plane), F32),
        in_specs=[vmem] * 5 + [smem] * 3 + [hbm] * 4,
        out_specs=vmem,
        scratch_shapes=[
            V(place.shape, BF16), V(spread.shape, BF16), V(win.shape, F32), V(win_out.shape, F32), dma((4,)),
            V((rows, cin * depth), F32), V((2, 2 * PAD, 6 * PAD), F32), V((rows, rows), F32), V((3, 2 * rows), F32),
            V((3, 3, rows, plane), BF16), V((2, rows, plane), BF16), V((2 * rows, plane), BF16),
            V((16, 24, LANES), F32), V((16, 32, LANES), F32),
            V((2, LANES), jnp.int32), V((n, 2, LANES), jnp.int32), V((1, LANES), jnp.int32),
            pltpu.SMEM((1, LANES), jnp.int32), dma, dma((n - 1,)), dma((n - 1,)),
            *exchange,
            dma((2,)), dma((2,)), dma((2, chips - 1)), dma((2, chips - 1)),
        ],
        compiler_params=pltpu.CompilerParams(
            collective_id=0, has_side_effects=True, vmem_limit_bytes=48 * 1024 * 1024
        ),
        cost_estimate=pl.CostEstimate(flops=6_000_000_000, bytes_accessed=8_000_000, transcendentals=110_592),
    )(features, w_in, w_plane, w_depth, w_head, brick_owner, patch_anchor, aug_code, place, spread, win, win_out)


def solution(mesh):
    in_specs = (
        P(("group", "patch"), None, None, None),
        P(),
        P(),
        P(),
        P(),
        P(("group", "patch")),
        P(("group", "patch")),
        P(("group", "patch")),
    )
    out_specs = P(("group", "patch"), None, None)
    return jax.shard_map(
        on_device, mesh=mesh, in_specs=in_specs, out_specs=out_specs, check_vma=False
    )
```

time: 95.4 us -> 30.7 us (0.32)
  blocking collectives: 33.6 us -> 0 us
  matrix products: 25.6 us -> 0 us
  Pallas kernels: 0 us -> 20.3 us
  local copies, waits for them, and re-layouts: 27.7 us -> 8.03 us
  other arithmetic: 5.69 us -> 0 us
    dot_general x14 -> x0, matrix products: 25.6 us -> none  [the longest x9 14.6 us: patch_output(): jnp.einsum('oi,izp->ozp', w_plane[3 * row_tap + col_tap], shifted_in, pre...]
    pallas_call x0 -> x1, Pallas kernels: none -> 20.3 us  [on_device(): pl.pallas_call(functools.partial(kernel, n, half), out_shape=jax.ShapeDty...]
    all_to_all x1 -> x0, blocking collectives: 19.8 us -> none  [on_device(): lax.all_to_all(departing_pieces, 'patch', split_axis=0, concat_axis=0, ti...]
    unnamed x1 -> x0, blocking collectives: 13.7 us -> none
    reshape x3 -> x0, local copies, waits for them, and re-layouts: 11.2 us -> none  [the longest x1 7.54 us: patch_output(): upsampled = upsampled.reshape(hidden, patch_depth, plane_side * plane_side)]
    broadcast_in_dim x2 -> x0, local copies, waits for them, and re-layouts: 9.15 us -> none  [patch_output(): jnp.broadcast_to(coarse_grid, (hidden, patch_depth, half_side, 2, half_si...]
    unnamed x26 -> x17, local copies, waits for them, and re-layouts: 2.93 us -> 8.03 us
    concatenate x2 -> x0, local copies, waits for them, and re-layouts: 2.48 us -> none  [patch_output(): weighted = jnp.concatenate([weighted, window[None]], axis=0)]
where the time goes in v1:
time: 30.7 us; the launch traced here: 30.3 us
  Pallas kernels  20.3 us (66%)
  local copies, waits for them, and re-layouts  8.03 us (26%)
  between operations  1.97 us (6%)
    pallas_call x1, Pallas kernels, on_device(): pl.pallas_call(functools.partial(kernel, n, half), out_shape=jax.ShapeDty...  20.3 us
    unnamed x17, local copies, waits for them, and re-layouts  8.03 us

profile of v1, /device:TPU:0, one launch (start us, length us, event | category | flops | bytes accessed | tf_op | source)
XLA Modules:
  0.0 30.3 jit_solution(16848743103011429824)
XLA Ops:
  1.9 0.0 copy-start
  2.0 1.3 %copy-done = bf16[1,64,4,2304]{3,2,1,0:T(4,128)(2,1)S(1)} copy-done((bf16[1,64,4,2304]{3,2,1,0:T(4,128)(2,1)S(1)}, bf16[1,64,4,2304]{3,2,1,0:T(4,128)(2,1)}, u32[]{:S(2)}) %copy-start) | copy-done | bytes 1179672
  3.2 0.0 copy-start.1
  3.2 0.9 %copy-done.1 = bf16[9,28,28]{2,1,0:T(8,128)(2,1)S(1)} copy-done((bf16[9,28,28]{2,1,0:T(8,128)(2,1)S(1)}, bf16[9,28,28]{2,1,0:T(8,128)(2,1)}, u32[]{:S(2)}) %copy-start.1) | copy-done | bytes 14136
  4.1 0.0 copy-start.2
  4.1 0.7 %copy-done.2 = bf16[3,28,28]{2,1,0:T(8,128)(2,1)S(1)} copy-done((bf16[3,28,28]{2,1,0:T(8,128)(2,1)S(1)}, bf16[3,28,28]{2,1,0:T(8,128)(2,1)}, u32[]{:S(2)}) %copy-start.2) | copy-done | bytes 4728
  4.8 0.0 copy-start.3
  4.8 0.7 %copy-done.3 = bf16[28,64]{1,0:T(8,128)(2,1)S(1)} copy-done((bf16[28,64]{1,0:T(8,128)(2,1)S(1)}, bf16[28,64]{1,0:T(8,128)(2,1)}, u32[]{:S(2)}) %copy-start.3) | copy-done | bytes 3608
  5.5 0.0 copy-start.4
  5.5 0.7 %copy-done.4 = bf16[3,28]{1,0:T(4,128)(2,1)S(1)} copy-done((bf16[3,28]{1,0:T(4,128)(2,1)S(1)}, bf16[3,28]{1,0:T(4,128)(2,1)}, u32[]{:S(2)}) %copy-start.4) | copy-done | bytes 192
  6.2 0.0 copy-start.5
  6.2 1.3 %copy-done.5 = bf16[2,512,576]{2,1,0:T(8,128)(2,1)S(1)} copy-done((bf16[2,512,576]{2,1,0:T(8,128)(2,1)S(1)}, bf16[2,512,576]{2,1,0:T(8,128)(2,1)}, u32[]{:S(2)}) %copy-start.5) | copy-done | bytes 1179672
  7.5 0.0 copy-start.6
  7.5 0.9 %copy-done.6 = f32[16,24,128]{2,1,0:T(8,128)S(1)} copy-done((f32[16,24,128]{2,1,0:T(8,128)S(1)}, f32[16,24,128]{2,1,0:T(8,128)}, u32[]{:S(2)}) %copy-start.6) | copy-done | bytes 196632
  8.5 0.0 copy-start.7
  8.5 0.9 %copy-done.7 = f32[16,1,2304]{2,1,0:T(1,128)S(1)} copy-done((f32[16,1,2304]{2,1,0:T(1,128)S(1)}, f32[16,1,2304]{2,1,0:T(1,128)}, u32[]{:S(2)}) %copy-start.7) | copy-done | bytes 147480
  9.4 20.3 %shard_map.118 = f32[1,4,2304]{2,1,0:T(4,128)S(1)} custom-call(bf16[1,64,4,2304]{3,2,1,0:T(4,128)(2,1)S(1)} %copy-done, bf16[28,64]{1,0:T(8,128)(2,1)S(1)} %copy-done.3, bf16[9,28,28]{2,1,0:T(8,128)(2,1)S(1)} %copy-done.1, bf16[3,28,28]{2,1,0:T(8,128)(2,1)S(1)} %copy-done.2, bf16[3,28]{1,0:T(4,128)(2,1)S(1)} %copy-done.4, s32[1]{0:T(128)S(6)} %copy.14.owner_s, ...), custom_call_target="tpu_custom_call" | custom-call | flops 6000000000 | bytes 8000000 | tf_op jit(solution)/shard_map/pallas_call | solution.py:348
  29.7 0.6 %copy.17 = f32[1,4,2304]{2,1,0:T(4,128)} copy(f32[1,4,2304]{2,1,0:T(4,128)S(1)} %shard_map.118) | data formatting | bytes 73728
Async XLA Ops:
  1.9 1.3 %copy-start = (bf16[1,64,4,2304]{3,2,1,0:T(4,128)(2,1)S(1)}, bf16[1,64,4,2304]{3,2,1,0:T(4,128)(2,1)}, u32[]{:S(2)}) copy-start(bf16[1,64,4,2304]{3,2,1,0:T(4,128)(2,1)} %feat.1) | copy-start | bytes 3538948
  3.2 0.9 %copy-start.1 = (bf16[9,28,28]{2,1,0:T(8,128)(2,1)S(1)}, bf16[9,28,28]{2,1,0:T(8,128)(2,1)}, u32[]{:S(2)}) copy-start(bf16[9,28,28]{2,1,0:T(8,128)(2,1)} %w_plane.1) | copy-start | bytes 42340
  4.1 0.7 %copy-start.2 = (bf16[3,28,28]{2,1,0:T(8,128)(2,1)S(1)}, bf16[3,28,28]{2,1,0:T(8,128)(2,1)}, u32[]{:S(2)}) copy-start(bf16[3,28,28]{2,1,0:T(8,128)(2,1)} %w_depth.1) | copy-start | bytes 14116
  4.8 0.7 %copy-start.3 = (bf16[28,64]{1,0:T(8,128)(2,1)S(1)}, bf16[28,64]{1,0:T(8,128)(2,1)}, u32[]{:S(2)}) copy-start(bf16[28,64]{1,0:T(8,128)(2,1)} %w_in.1) | copy-start | bytes 10756
  5.5 0.7 %copy-start.4 = (bf16[3,28]{1,0:T(4,128)(2,1)S(1)}, bf16[3,28]{1,0:T(4,128)(2,1)}, u32[]{:S(2)}) copy-start(bf16[3,28]{1,0:T(4,128)(2,1)} %w_head.1) | copy-start | bytes 508
  6.2 1.3 %copy-start.5 = (bf16[2,512,576]{2,1,0:T(8,128)(2,1)S(1)}, bf16[2,512,576]{2,1,0:T(8,128)(2,1)}, u32[]{:S(2)}) copy-start(bf16[2,512,576]{2,1,0:T(8,128)(2,1)} %constant.9.clone.spread_h) | copy-start | bytes 3538948
  7.5 0.9 %copy-start.6 = (f32[16,24,128]{2,1,0:T(8,128)S(1)}, f32[16,24,128]{2,1,0:T(8,128)}, u32[]{:S(2)}) copy-start(f32[16,24,128]{2,1,0:T(8,128)} %constant.10.clone.win_h) | copy-start | bytes 589828
  8.5 0.9 %copy-start.7 = (f32[16,1,2304]{2,1,0:T(1,128)S(1)}, f32[16,1,2304]{2,1,0:T(1,128)}, u32[]{:S(2)}) copy-start(f32[16,1,2304]{2,1,0:T(1,128)} %constant.11.clone.win_out_h) | copy-start | bytes 442372

commit v2 on v1

--- a/solution.py
+++ b/solution.py
@@ -11,6 +11,7 @@
 
 MESH = pl.DeviceIdType.MESH
 LANES = 128
+TILE = 256
 PAD = 32
 F32 = jnp.float32
 BF16 = jnp.bfloat16
@@ -90,8 +91,9 @@
 
 def kernel(
     n, half,
-    feat, w_in, w_plane, w_depth, w_head, owner_s, anchor_s, code_s, place_h, spread_h, win_h, win_out_h,
+    feat_h, w_in_h, w_plane_h, w_depth_h, w_head_h, owner_h, anchor_h, code_h, place_h, spread_h, win_h, win_out_h,
     out,
+    feat, w_in, w_plane, w_depth, w_head, owner_s, anchor_s, code_s, arg_sem,
     place, spread, win, win_out, table_sem,
     wi_s, wp_s, wd_s, wh_s, xs, first_s, second_s, br0, br1,
     say, heard, inverse_v, inverse_s, inverse_sem, say_sem, hear_sem,
@@ -111,7 +113,19 @@
     me = lax.axis_index("patch")
     chip, core = me // 2, lax.rem(me, 2)
     partner = me + 1 - 2 * core
-
+    tiles = [slice(at, at + TILE) for at in range(0, plane, TILE)]
+
+    arguments = [
+        pltpu.make_async_copy(h, v, arg_sem.at[s])
+        for s, (h, v) in enumerate(
+            (
+                (owner_h, owner_s), (anchor_h, anchor_s), (code_h, code_s), (w_in_h, w_in),
+                (w_plane_h, w_plane), (w_depth_h, w_depth), (w_head_h, w_head), (feat_h, feat),
+            )
+        )
+    ]
+    for argument in arguments:
+        argument.start()
     loads = [
         pltpu.make_async_copy(h, v, table_sem.at[s])
         for s, (h, v) in enumerate(((place_h, place), (win_h, win), (spread_h, spread), (win_out_h, win_out)))
@@ -123,6 +137,8 @@
     for off in range(1, n):
         pl.semaphore_signal(barrier, inc=1, device_id={"patch": lax.rem(me + off, n)}, device_id_type=MESH)
 
+    for argument in arguments[:7]:
+        argument.wait()
     code = code_s[0]
     anchor = anchor_s[0]
     fz, fy, fx = code % 2, (code // 2) % 2, code // 4
@@ -150,9 +166,9 @@
                     col = PAD * (3 * dyi + px + at)
                     wp_s[sy, PAD * px : PAD * px + hidden, col : col + hidden] = total
     wd_s[...] = jnp.zeros_like(wd_s)
-    for z in range(depth):
+    for z in range(2 * depth):
         for tz in range(3):
-            if 0 <= z + tz - 1 < depth:
+            if (z + tz - 1) // depth == z // depth:
                 col = PAD * (z + tz - 1)
                 wd_s[PAD * z : PAD * z + hidden, col : col + hidden] = w_depth[tz].astype(F32)
     wh_s[...] = jnp.zeros_like(wh_s)
@@ -168,7 +184,12 @@
     ).astype(BF16)
     depth_w = wd_s[...].astype(BF16)
 
-    x = dot(wi_s[...].astype(BF16), feat[0].reshape(cin * depth, plane)).astype(BF16)
+    project = wi_s[...].astype(BF16)
+    arguments[7].wait()
+    parts = []
+    for cols in tiles:
+        parts.append(dot(project, feat[0, :, :, cols].reshape(cin * depth, TILE)).astype(BF16))
+    x = jnp.concatenate(parts, axis=1)
     lane_x = lax.broadcasted_iota(jnp.int32, (1, plane), 1) % half
     left = shifted(x, -1) * (lane_x >= 1).astype(F32).astype(BF16)
     right = shifted(x, 1) * (lane_x <= half - 2).astype(F32).astype(BF16)
@@ -194,23 +215,28 @@
         sy = jnp.where(fy == 1, 1 - qy, qy)
         w_high, w_low = split(wp_s[sy])
         weights = jnp.concatenate([w_high, w_low], axis=0)
-        around = [xs[sy + dyi, dx] for dyi in range(2) for dx in range(3)]
-        for z in range(depth):
-            rows = slice(PAD * z, PAD * (z + 1))
-            mixed = dot(weights, jnp.concatenate([a[rows] for a in around], axis=0))
-            mixed = mixed[: 2 * PAD] + mixed[2 * PAD :]
-            up = xs[1, 1, rows, :].astype(F32)
-            for px in range(2):
-                first = up + jnp.maximum(mixed[PAD * px : PAD * (px + 1)], 0.0)
-                first_s[px, rows, :] = first.astype(BF16)
+        for cols in tiles:
+            for z in range(depth):
+                rows = slice(PAD * z, PAD * (z + 1))
+                around = [xs[sy + dyi, dx, rows, cols] for dyi in range(2) for dx in range(3)]
+                mixed = dot(weights, jnp.concatenate(around, axis=0))
+                mixed = mixed[: 2 * PAD] + mixed[2 * PAD :]
+                up = xs[1, 1, rows, cols].astype(F32)
+                for px in range(2):
+                    first = up + jnp.maximum(mixed[PAD * px : PAD * (px + 1)], 0.0)
+                    at = PAD * (depth * px + z)
+                    first_s[at : at + PAD, cols] = first.astype(BF16)
 
     def heads(qy, brick):
-        for px in range(2):
-            first = first_s[px]
+        for cols in tiles:
+            first = first_s[:, cols]
             second = first.astype(F32) + jnp.maximum(dot(depth_w, first), 0.0)
-            second_s[depth * PAD * px : depth * PAD * (px + 1), :] = second.astype(BF16)
-        affinity = jax.nn.sigmoid(dot(head, second_s[...]))
-        both = jnp.concatenate(split(affinity), axis=0)
+            second_s[:, cols] = second.astype(BF16)
+        both = []
+        for cols in tiles:
+            affinity = jax.nn.sigmoid(dot(head, second_s[:, cols]))
+            both.append(jnp.concatenate(split(affinity), axis=0))
+        both = jnp.concatenate(both, axis=1)
         stacked = jnp.concatenate([both[:, block * i : block * (i + 1)] for i in range(4)], axis=0)
         if qy == 0:
             loads[0].wait()
@@ -337,7 +363,6 @@
     chips = n // 2
     place, spread, win, win_out = tables(half, depth)
     vmem = pl.BlockSpec(memory_space=pltpu.VMEM)
-    smem = pl.BlockSpec(memory_space=pltpu.SMEM)
     hbm = pl.BlockSpec(memory_space=pl.ANY)
     rows = depth * PAD
     V = pltpu.VMEM
@@ -348,12 +373,14 @@
     return pl.pallas_call(
         functools.partial(kernel, n, half),
         out_shape=jax.ShapeDtypeStruct((1, 4, plane), F32),
-        in_specs=[vmem] * 5 + [smem] * 3 + [hbm] * 4,
+        in_specs=[hbm] * 12,
         out_specs=vmem,
         scratch_shapes=[
+            V(features.shape, BF16), V(w_in.shape, BF16), V(w_plane.shape, BF16), V(w_depth.shape, BF16),
+            V(w_head.shape, BF16), *[pltpu.SMEM((1,), jnp.int32)] * 3, dma((8,)),
             V(place.shape, BF16), V(spread.shape, BF16), V(win.shape, F32), V(win_out.shape, F32), dma((4,)),
-            V((rows, cin * depth), F32), V((2, 2 * PAD, 6 * PAD), F32), V((rows, rows), F32), V((3, 2 * rows), F32),
-            V((3, 3, rows, plane), BF16), V((2, rows, plane), BF16), V((2 * rows, plane), BF16),
+            V((rows, cin * depth), F32), V((2, 2 * PAD, 6 * PAD), F32), V((2 * rows, 2 * rows), F32), V((3, 2 * rows), F32),
+            V((3, 3, rows, plane), BF16), V((2 * rows, plane), BF16), V((2 * rows, plane), BF16),
             V((16, 24, LANES), F32), V((16, 32, LANES), F32),
             V((2, LANES), jnp.int32), V((n, 2, LANES), jnp.int32), V((1, LANES), jnp.int32),
             pltpu.SMEM((1, LANES), jnp.int32), dma, dma((n - 1,)), dma((n - 1,)),

time: 30.7 us -> 31.4 us (1.023)
  Pallas kernels: 20.3 us -> 21 us
    pallas_call x1, Pallas kernels: 20.3 us -> 21 us  [on_device(): pl.pallas_call(functools.partial(kernel, n, half), out_shape=jax.ShapeDty...]
where the time goes in v2:
time: 31.4 us; the launch traced here: 31 us
  Pallas kernels  21 us (67%)
  local copies, waits for them, and re-layouts  8.03 us (26%)
  between operations  1.97 us (6%)
    pallas_call x1, Pallas kernels, on_device(): pl.pallas_call(functools.partial(kernel, n, half), out_shape=jax.ShapeDty...  21 us
    unnamed x17, local copies, waits for them, and re-layouts  8.03 us

profile of v2, /device:TPU:0, one launch (start us, length us, event | category | flops | bytes accessed | tf_op | source)
XLA Modules:
  0.0 31.0 jit_solution(7528346819174254706)
XLA Ops:
  1.9 0.0 copy-start
  2.0 1.3 %copy-done = bf16[1,64,4,2304]{3,2,1,0:T(4,128)(2,1)S(1)} copy-done((bf16[1,64,4,2304]{3,2,1,0:T(4,128)(2,1)S(1)}, bf16[1,64,4,2304]{3,2,1,0:T(4,128)(2,1)}, u32[]{:S(2)}) %copy-start) | copy-done | bytes 1179672
  3.2 0.0 copy-start.1
  3.2 0.9 %copy-done.1 = bf16[9,28,28]{2,1,0:T(8,128)(2,1)S(1)} copy-done((bf16[9,28,28]{2,1,0:T(8,128)(2,1)S(1)}, bf16[9,28,28]{2,1,0:T(8,128)(2,1)}, u32[]{:S(2)}) %copy-start.1) | copy-done | bytes 14136
  4.1 0.0 copy-start.2
  4.1 0.7 %copy-done.2 = bf16[3,28,28]{2,1,0:T(8,128)(2,1)S(1)} copy-done((bf16[3,28,28]{2,1,0:T(8,128)(2,1)S(1)}, bf16[3,28,28]{2,1,0:T(8,128)(2,1)}, u32[]{:S(2)}) %copy-start.2) | copy-done | bytes 4728
  4.8 0.0 copy-start.3
  4.8 0.7 %copy-done.3 = bf16[28,64]{1,0:T(8,128)(2,1)S(1)} copy-done((bf16[28,64]{1,0:T(8,128)(2,1)S(1)}, bf16[28,64]{1,0:T(8,128)(2,1)}, u32[]{:S(2)}) %copy-start.3) | copy-done | bytes 3608
  5.5 0.0 copy-start.4
  5.5 0.7 %copy-done.4 = bf16[3,28]{1,0:T(4,128)(2,1)S(1)} copy-done((bf16[3,28]{1,0:T(4,128)(2,1)S(1)}, bf16[3,28]{1,0:T(4,128)(2,1)}, u32[]{:S(2)}) %copy-start.4) | copy-done | bytes 192
  6.2 0.0 copy-start.5
  6.2 1.3 %copy-done.5 = bf16[2,512,576]{2,1,0:T(8,128)(2,1)S(1)} copy-done((bf16[2,512,576]{2,1,0:T(8,128)(2,1)S(1)}, bf16[2,512,576]{2,1,0:T(8,128)(2,1)}, u32[]{:S(2)}) %copy-start.5) | copy-done | bytes 1179672
  7.5 0.0 copy-start.6
  7.5 0.9 %copy-done.6 = f32[16,24,128]{2,1,0:T(8,128)S(1)} copy-done((f32[16,24,128]{2,1,0:T(8,128)S(1)}, f32[16,24,128]{2,1,0:T(8,128)}, u32[]{:S(2)}) %copy-start.6) | copy-done | bytes 196632
  8.5 0.0 copy-start.7
  8.5 0.9 %copy-done.7 = f32[16,1,2304]{2,1,0:T(1,128)S(1)} copy-done((f32[16,1,2304]{2,1,0:T(1,128)S(1)}, f32[16,1,2304]{2,1,0:T(1,128)}, u32[]{:S(2)}) %copy-start.7) | copy-done | bytes 147480
  9.4 21.0 %shard_map.118 = f32[1,4,2304]{2,1,0:T(4,128)S(1)} custom-call(bf16[1,64,4,2304]{3,2,1,0:T(4,128)(2,1)S(1)} %copy-done, bf16[28,64]{1,0:T(8,128)(2,1)S(1)} %copy-done.3, bf16[9,28,28]{2,1,0:T(8,128)(2,1)S(1)} %copy-done.1, bf16[3,28,28]{2,1,0:T(8,128)(2,1)S(1)} %copy-done.2, bf16[3,28]{1,0:T(4,128)(2,1)S(1)} %copy-done.4, s32[1]{0:T(128)S(6)} %copy.14.owner_h, ...), custom_call_target="tpu_custom_call" | custom-call | flops 6000000000 | bytes 8000000 | tf_op jit(solution)/shard_map/pallas_call | solution.py:373
  30.3 0.6 %copy.17 = f32[1,4,2304]{2,1,0:T(4,128)} copy(f32[1,4,2304]{2,1,0:T(4,128)S(1)} %shard_map.118) | data formatting | bytes 73728
Async XLA Ops:
  1.9 1.3 %copy-start = (bf16[1,64,4,2304]{3,2,1,0:T(4,128)(2,1)S(1)}, bf16[1,64,4,2304]{3,2,1,0:T(4,128)(2,1)}, u32[]{:S(2)}) copy-start(bf16[1,64,4,2304]{3,2,1,0:T(4,128)(2,1)} %feat_h.1) | copy-start | bytes 3538948
  3.2 0.9 %copy-start.1 = (bf16[9,28,28]{2,1,0:T(8,128)(2,1)S(1)}, bf16[9,28,28]{2,1,0:T(8,128)(2,1)}, u32[]{:S(2)}) copy-start(bf16[9,28,28]{2,1,0:T(8,128)(2,1)} %w_plane_h.1) | copy-start | bytes 42340
  4.1 0.7 %copy-start.2 = (bf16[3,28,28]{2,1,0:T(8,128)(2,1)S(1)}, bf16[3,28,28]{2,1,0:T(8,128)(2,1)}, u32[]{:S(2)}) copy-start(bf16[3,28,28]{2,1,0:T(8,128)(2,1)} %w_depth_h.1) | copy-start | bytes 14116
  4.8 0.7 %copy-start.3 = (bf16[28,64]{1,0:T(8,128)(2,1)S(1)}, bf16[28,64]{1,0:T(8,128)(2,1)}, u32[]{:S(2)}) copy-start(bf16[28,64]{1,0:T(8,128)(2,1)} %w_in_h.1) | copy-start | bytes 10756
  5.5 0.7 %copy-start.4 = (bf16[3,28]{1,0:T(4,128)(2,1)S(1)}, bf16[3,28]{1,0:T(4,128)(2,1)}, u32[]{:S(2)}) copy-start(bf16[3,28]{1,0:T(4,128)(2,1)} %w_head_h.1) | copy-start | bytes 508
  6.2 1.3 %copy-start.5 = (bf16[2,512,576]{2,1,0:T(8,128)(2,1)S(1)}, bf16[2,512,576]{2,1,0:T(8,128)(2,1)}, u32[]{:S(2)}) copy-start(bf16[2,512,576]{2,1,0:T(8,128)(2,1)} %constant.9.clone.spread_h) | copy-start | bytes 3538948
  7.5 0.9 %copy-start.6 = (f32[16,24,128]{2,1,0:T(8,128)S(1)}, f32[16,24,128]{2,1,0:T(8,128)}, u32[]{:S(2)}) copy-start(f32[16,24,128]{2,1,0:T(8,128)} %constant.10.clone.win_h) | copy-start | bytes 589828
  8.5 0.9 %copy-start.7 = (f32[16,1,2304]{2,1,0:T(1,128)S(1)}, f32[16,1,2304]{2,1,0:T(1,128)}, u32[]{:S(2)}) copy-start(f32[16,1,2304]{2,1,0:T(1,128)} %constant.11.clone.win_out_h) | copy-start | bytes 442372

commit v3 on v2

--- a/solution.py
+++ b/solution.py
@@ -50,7 +50,7 @@
             for g in range(groups):
                 spread[py, (2 + px) * LANES + rest * g + np.arange(rest), cell[LANES:]] = 1
     bz, by = bump(depth), bump(side)
-    win = np.zeros((16, 24, LANES), np.float32)
+    win = np.zeros((17, 24, LANES), np.float32)
     win_out = np.zeros((16, 1, depth * fine), np.float32)
     for i in range(4):
         for j in range(4):
@@ -130,9 +130,6 @@
         pltpu.make_async_copy(h, v, table_sem.at[s])
         for s, (h, v) in enumerate(((place_h, place), (win_h, win), (spread_h, spread), (win_out_h, win_out)))
     ]
-    for load in loads:
-        load.start()
-
     barrier = pltpu.get_barrier_semaphore()
     for off in range(1, n):
         pl.semaphore_signal(barrier, inc=1, device_id={"patch": lax.rem(me + off, n)}, device_id_type=MESH)
@@ -186,6 +183,8 @@
 
     project = wi_s[...].astype(BF16)
     arguments[7].wait()
+    for load in loads:
+        load.start()
     parts = []
     for cols in tiles:
         parts.append(dot(project, feat[0, :, :, cols].reshape(cin * depth, TILE)).astype(BF16))
@@ -254,47 +253,50 @@
                     br1[e, 24:32, :] = br1[e, 24:32, :] + tail
 
     def piece(qy, brick, v):
-        b = inverse_s[0, v]
-        i = lax.rem(b // 4 - anchor + brick_rows, brick_rows)
-        valid = (i < 4).astype(F32)
-        i = jnp.minimum(i, 3)
-        j = lax.rem(b, 4)
-        source = jnp.where(fy == 1, 3 - i, i)
-        window = win[4 * i + j]
+        window = win[inverse_s[2, v]]
         part = window[8 * qy : 8 * qy + 8]
         window = jnp.concatenate([part] * 3 + ([window[16:24]] if qy else []), axis=0)
-        return brick[4 * source + j] * window * valid
+        return brick[inverse_s[1, v]] * window
+
+    cut = chips // 2
+    spans = (slice(0, cut), slice(cut, chips))
 
     def pair_start(qy, brick, pair_out, pair_in, kept):
-        for t in range(chips):
-            pair_out[t] = piece(qy, brick, 2 * t + 1 - core)
-        copy = pltpu.make_async_remote_copy(
-            src_ref=pair_out, dst_ref=pair_in, send_sem=pair_send.at[qy], recv_sem=pair_recv.at[qy],
-            device_id={"patch": partner}, device_id_type=MESH,
-        )
-        copy.start()
-        for t in range(chips):
-            kept[t] = piece(qy, brick, 2 * t + core)
-        return copy
-
-    def cross_start(qy, copy, pair_in, kept, cross_out, cross_in):
-        copy.wait()
         copies = []
-        for off in range(1, chips):
-            t = lax.rem(chip + off, chips)
-            cross_out[off - 1] = kept[t] + pair_in[t]
+        for part, span in enumerate(spans):
+            for slot in range(span.start, span.stop):
+                pair_out[slot] = piece(qy, brick, 2 * lax.rem(chip + slot + 1, chips) + 1 - core)
+            window = pl.ds(span.start, span.stop - span.start)
             copies.append(
                 pltpu.make_async_remote_copy(
-                    src_ref=cross_out.at[off - 1], dst_ref=cross_in.at[off - 1],
-                    send_sem=cross_send.at[qy, off - 1], recv_sem=cross_recv.at[qy, off - 1],
-                    device_id={"patch": 2 * t + core}, device_id_type=MESH,
+                    src_ref=pair_out.at[window], dst_ref=pair_in.at[window],
+                    send_sem=pair_send.at[qy, part], recv_sem=pair_recv.at[qy, part],
+                    device_id={"patch": partner}, device_id_type=MESH,
                 )
             )
             copies[-1].start()
+        for slot in range(chips):
+            kept[slot] = piece(qy, brick, 2 * lax.rem(chip + slot + 1, chips) + core)
         return copies
 
+    def cross_start(qy, pairs, pair_in, kept, cross_out, cross_in):
+        copies = []
+        for pair, span in zip(pairs, spans):
+            pair.wait()
+            for slot in range(span.start, min(span.stop, chips - 1)):
+                cross_out[slot] = kept[slot] + pair_in[slot]
+                copies.append(
+                    pltpu.make_async_remote_copy(
+                        src_ref=cross_out.at[slot], dst_ref=cross_in.at[slot],
+                        send_sem=cross_send.at[qy, slot], recv_sem=cross_recv.at[qy, slot],
+                        device_id={"patch": 2 * lax.rem(chip + slot + 1, chips) + core}, device_id_type=MESH,
+                    )
+                )
+                copies[-1].start()
+        return copies
+
     def cross_end(copies, pair_in, kept, cross_in):
-        total = kept[chip] + pair_in[chip]
+        total = kept[chips - 1] + pair_in[chips - 1]
         for at, copy in enumerate(copies):
             copy.wait()
             total = total + cross_in[at]
@@ -304,7 +306,15 @@
     for tell in tells:
         tell.wait()
     lane1 = lax.broadcasted_iota(jnp.int32, (1, LANES), 1)
-    inverse_v[...] = sum(jnp.where(heard[d, 0:1, :] == lane1, d, 0) for d in range(n))
+    inverse = sum(jnp.where(heard[d, 0:1, :] == lane1, d, 0) for d in range(n))
+    i = inverse // 4 - anchor
+    i = jnp.where(i < 0, i + brick_rows, i)
+    j = inverse % 4
+    held_i = jnp.minimum(i, 3)
+    inverse_v[0:1, :] = inverse
+    inverse_v[1:2, :] = 4 * jnp.where(fy == 1, 3 - held_i, held_i) + j
+    inverse_v[2:3, :] = jnp.where(i < 4, 4 * held_i + j, 16)
+    inverse_v[3:8, :] = jnp.zeros((5, LANES), jnp.int32)
     fetch = pltpu.make_async_copy(inverse_v, inverse_s, inverse_sem)
     fetch.start()
     heads(0, br0)
@@ -363,7 +373,7 @@
     chips = n // 2
     place, spread, win, win_out = tables(half, depth)
     vmem = pl.BlockSpec(memory_space=pltpu.VMEM)
-    hbm = pl.BlockSpec(memory_space=pl.ANY)
+    hbm = pl.BlockSpec(memory_space=pltpu.HBM)
     rows = depth * PAD
     V = pltpu.VMEM
     dma = pltpu.SemaphoreType.DMA
@@ -382,13 +392,13 @@
             V((rows, cin * depth), F32), V((2, 2 * PAD, 6 * PAD), F32), V((2 * rows, 2 * rows), F32), V((3, 2 * rows), F32),
             V((3, 3, rows, plane), BF16), V((2 * rows, plane), BF16), V((2 * rows, plane), BF16),
             V((16, 24, LANES), F32), V((16, 32, LANES), F32),
-            V((2, LANES), jnp.int32), V((n, 2, LANES), jnp.int32), V((1, LANES), jnp.int32),
-            pltpu.SMEM((1, LANES), jnp.int32), dma, dma((n - 1,)), dma((n - 1,)),
+            V((2, LANES), jnp.int32), V((n, 2, LANES), jnp.int32), V((8, LANES), jnp.int32),
+            pltpu.SMEM((8, LANES), jnp.int32), dma, dma((n - 1,)), dma((n - 1,)),
             *exchange,
-            dma((2,)), dma((2,)), dma((2, chips - 1)), dma((2, chips - 1)),
+            dma((2, 2)), dma((2, 2)), dma((2, chips - 1)), dma((2, chips - 1)),
         ],
         compiler_params=pltpu.CompilerParams(
-            collective_id=0, has_side_effects=True, vmem_limit_bytes=48 * 1024 * 1024
+            collective_id=0, has_side_effects=True, vmem_limit_bytes=60 * 1024 * 1024
         ),
         cost_estimate=pl.CostEstimate(flops=6_000_000_000, bytes_accessed=8_000_000, transcendentals=110_592),
     )(features, w_in, w_plane, w_depth, w_head, brick_owner, patch_anchor, aug_code, place, spread, win, win_out)

time: 31.4 us -> 24.3 us (0.77)
  local copies, waits for them, and re-layouts: 8.03 us -> 1.39 us
    unnamed x17 -> x1, local copies, waits for them, and re-layouts: 8.03 us -> 1.39 us
where the time goes in v3:
time: 24.3 us; the launch traced here: 24 us
  Pallas kernels  20.7 us (85%)
  between operations  1.95 us (8%)
  local copies, waits for them, and re-layouts  1.39 us (6%)
    pallas_call x1, Pallas kernels, on_device(): pl.pallas_call(functools.partial(kernel, n, half), out_shape=jax.ShapeDty...  20.7 us
    unnamed x1, local copies, waits for them, and re-layouts  1.39 us

profile of v3, /device:TPU:0, one launch (start us, length us, event | category | flops | bytes accessed | tf_op | source)
XLA Modules:
  0.0 24.0 jit_solution(5025375845457172644)
XLA Ops:
  1.9 20.7 %shard_map.118 = f32[1,4,2304]{2,1,0:T(4,128)} custom-call(bf16[1,64,4,2304]{3,2,1,0:T(4,128)(2,1)} %feat_h.1, bf16[28,64]{1,0:T(8,128)(2,1)} %w_in_h.1, bf16[9,28,28]{2,1,0:T(8,128)(2,1)} %w_plane_h.1, bf16[3,28,28]{2,1,0:T(8,128)(2,1)} %w_depth_h.1, bf16[3,28]{1,0:T(4,128)(2,1)} %w_head_h.1, s32[1]{0:T(128)S(6)} %copy.14.owner_h, s32[1]{0:T(128)S(6)} %copy.15.anchor_h, ...), custom_call_target="tpu_custom_call" | custom-call | flops 6000000000 | bytes 8000000 | tf_op jit(solution)/shard_map/pallas_call | solution.py:383
  22.6 1.4 %copy.17 = f32[1,4,2304]{2,1,0:T(4,128)} copy(f32[1,4,2304]{2,1,0:T(4,128)} %shard_map.118) | data formatting | bytes 73728

commit v4 on v3

--- a/solution.py
+++ b/solution.py
@@ -134,8 +134,10 @@
     for off in range(1, n):
         pl.semaphore_signal(barrier, inc=1, device_id={"patch": lax.rem(me + off, n)}, device_id_type=MESH)
 
-    for argument in arguments[:7]:
+    for argument in arguments:
         argument.wait()
+    for load in loads:
+        load.start()
     code = code_s[0]
     anchor = anchor_s[0]
     fz, fy, fx = code % 2, (code // 2) % 2, code // 4
@@ -152,6 +154,19 @@
     wi_s[...] = jnp.zeros_like(wi_s)
     for z in range(depth):
         wi_s[PAD * z : PAD * z + hidden, :] = jnp.where(section == z, wi_all, 0.0)
+    project = wi_s[...].astype(BF16)
+    parts = []
+    for cols in tiles:
+        parts.append(dot(project, feat[0, :, :, cols].reshape(cin * depth, TILE)).astype(BF16))
+    x = jnp.concatenate(parts, axis=1)
+    lane_x = lax.broadcasted_iota(jnp.int32, (1, plane), 1) % half
+    left = shifted(x, -1) * (lane_x >= 1).astype(F32).astype(BF16)
+    right = shifted(x, 1) * (lane_x <= half - 2).astype(F32).astype(BF16)
+    for dx, values in enumerate((left, x, right)):
+        xs[0, dx] = shifted(values, -half)
+        xs[1, dx] = values
+        xs[2, dx] = shifted(values, half)
+
     wp_s[...] = jnp.zeros_like(wp_s)
     taps = [w_plane[t].astype(F32) for t in range(9)]
     halves = (((0,), (1, 2)), ((0, 1), (2,)))
@@ -181,22 +196,6 @@
     ).astype(BF16)
     depth_w = wd_s[...].astype(BF16)
 
-    project = wi_s[...].astype(BF16)
-    arguments[7].wait()
-    for load in loads:
-        load.start()
-    parts = []
-    for cols in tiles:
-        parts.append(dot(project, feat[0, :, :, cols].reshape(cin * depth, TILE)).astype(BF16))
-    x = jnp.concatenate(parts, axis=1)
-    lane_x = lax.broadcasted_iota(jnp.int32, (1, plane), 1) % half
-    left = shifted(x, -1) * (lane_x >= 1).astype(F32).astype(BF16)
-    right = shifted(x, 1) * (lane_x <= half - 2).astype(F32).astype(BF16)
-    for dx, values in enumerate((left, x, right)):
-        xs[0, dx] = shifted(values, -half)
-        xs[1, dx] = values
-        xs[2, dx] = shifted(values, half)
-
     pl.semaphore_wait(barrier, n - 1)
     tells = []
     for off in range(1, n):
@@ -340,25 +339,23 @@
         window = window + count[:, 0:1] * win_out[4 * i + lax.rem(mine, 4)]
     out[0, 3:4, :] = window
 
-    totals = (
-        cross_end(cross0, pair_in0, kept0, cross_in0),
-        cross_end(cross1, pair_in1, kept1, cross_in1),
-    )
-    tail = totals[1][24:32]
     right_px = lax.broadcasted_iota(jnp.int32, (24, LANES), 0) // 4 % 2 == 1
-    result = jnp.zeros((24, fine), F32)
-    for py in range(2):
-        main = totals[py][0:24]
-        tails = jnp.concatenate([jnp.where(lane == 3 * py + k, tail, 0.0) for k in range(3)], axis=0)
-        wide = jnp.concatenate(
-            [
-                jnp.where(right_px, 0.0, main), jnp.where(right_px, main, 0.0),
-                jnp.where(right_px, 0.0, tails), jnp.where(right_px, tails, 0.0),
-            ],
-            axis=1,
-        )
-        both = dot(jnp.concatenate(split(wide), axis=0), spread[py])
-        result = result + (both[:24] + both[24:])
+
+    def by_px(values):
+        return [jnp.where(right_px, 0.0, values), jnp.where(right_px, values, 0.0)]
+
+    def put(values, spreading):
+        both = dot(jnp.concatenate(split(jnp.concatenate(values, axis=1)), axis=0), spreading)
+        return both[:24] + both[24:]
+
+    result = put(by_px(cross_end(cross0, pair_in0, kept0, cross_in0)), spread[0, 0 : 2 * LANES, :])
+    total = cross_end(cross1, pair_in1, kept1, cross_in1)
+    tail = total[24:32]
+    tails = [
+        jnp.concatenate([jnp.where(lane == 3 * py + k, tail, 0.0) for k in range(3)], axis=0) for py in range(2)
+    ]
+    result = result + put(by_px(tails[0]), spread[0, 2 * LANES :, :])
+    result = result + put(by_px(total[0:24]) + by_px(tails[1]), spread[1])
     for k in range(3):
         for z in range(depth):
             row = 8 * k + z

time: 24.3 us -> 24.2 us (level)
  no operation moved by 1% of the time
where the time goes in v4:
time: 24.2 us; the launch traced here: 24 us
  Pallas kernels  20.7 us (86%)
  between operations  1.95 us (8%)
  local copies, waits for them, and re-layouts  1.39 us (6%)
    pallas_call x1, Pallas kernels, on_device(): pl.pallas_call(functools.partial(kernel, n, half), out_shape=jax.ShapeDty...  20.7 us
    unnamed x1, local copies, waits for them, and re-layouts  1.39 us

profile of v4, /device:TPU:0, one launch (start us, length us, event | category | flops | bytes accessed | tf_op | source)
XLA Modules:
  0.0 24.0 jit_solution(8767117416160622938)
XLA Ops:
  1.9 20.7 %shard_map.118 = f32[1,4,2304]{2,1,0:T(4,128)} custom-call(bf16[1,64,4,2304]{3,2,1,0:T(4,128)(2,1)} %feat_h.1, bf16[28,64]{1,0:T(8,128)(2,1)} %w_in_h.1, bf16[9,28,28]{2,1,0:T(8,128)(2,1)} %w_plane_h.1, bf16[3,28,28]{2,1,0:T(8,128)(2,1)} %w_depth_h.1, bf16[3,28]{1,0:T(4,128)(2,1)} %w_head_h.1, s32[1]{0:T(128)S(6)} %copy.14.owner_h, s32[1]{0:T(128)S(6)} %copy.15.anchor_h, ...), custom_call_target="tpu_custom_call" | custom-call | flops 6000000000 | bytes 8000000 | tf_op jit(solution)/shard_map/pallas_call | solution.py:380
  22.6 1.4 %copy.17 = f32[1,4,2304]{2,1,0:T(4,128)} copy(f32[1,4,2304]{2,1,0:T(4,128)} %shard_map.118) | data formatting | bytes 73728

commit v5 on v4

--- a/solution.py
+++ b/solution.py
@@ -115,12 +115,14 @@
     partner = me + 1 - 2 * core
     tiles = [slice(at, at + TILE) for at in range(0, plane, TILE)]
 
+    quarters = [pl.ds(at, cin // 4) for at in range(0, cin, cin // 4)]
     arguments = [
         pltpu.make_async_copy(h, v, arg_sem.at[s])
         for s, (h, v) in enumerate(
             (
                 (owner_h, owner_s), (anchor_h, anchor_s), (code_h, code_s), (w_in_h, w_in),
-                (w_plane_h, w_plane), (w_depth_h, w_depth), (w_head_h, w_head), (feat_h, feat),
+                (w_plane_h, w_plane), (w_depth_h, w_depth), (w_head_h, w_head),
+                *[(feat_h.at[:, some], feat.at[:, some]) for some in quarters],
             )
         )
     ]
@@ -128,7 +130,12 @@
         argument.start()
     loads = [
         pltpu.make_async_copy(h, v, table_sem.at[s])
-        for s, (h, v) in enumerate(((place_h, place), (win_h, win), (spread_h, spread), (win_out_h, win_out)))
+        for s, (h, v) in enumerate(
+            (
+                *[(place_h.at[flip], place.at[flip]) for flip in range(4)],
+                (win_h, win), (spread_h.at[0], spread.at[0]), (spread_h.at[1], spread.at[1]), (win_out_h, win_out),
+            )
+        )
     ]
     barrier = pltpu.get_barrier_semaphore()
     for off in range(1, n):
@@ -237,7 +244,8 @@
         both = jnp.concatenate(both, axis=1)
         stacked = jnp.concatenate([both[:, block * i : block * (i + 1)] for i in range(4)], axis=0)
         if qy == 0:
-            loads[0].wait()
+            for load in loads[:4]:
+                load.wait()
         placed = dot(stacked, place[code // 2])
         for i in range(4):
             value = placed[48 * i : 48 * i + 24] + placed[48 * i + 24 : 48 * i + 48]
@@ -318,7 +326,7 @@
     fetch.start()
     heads(0, br0)
     fetch.wait()
-    loads[1].wait()
+    loads[4].wait()
     pair0 = pair_start(0, br0, pair_out0, pair_in0, kept0)
     planes(1)
     cross0 = cross_start(0, pair0, pair_in0, kept0, cross_out0, cross_in0)
@@ -326,8 +334,8 @@
     pair1 = pair_start(1, br1, pair_out1, pair_in1, kept1)
     cross1 = cross_start(1, pair1, pair_in1, kept1, cross_out1, cross_in1)
 
-    loads[2].wait()
-    loads[3].wait()
+    for load in loads[5:]:
+        load.wait()
     mine = inverse_s[0, me]
     window = jnp.zeros((1, win_out.shape[2]), F32)
     for i in range(4):
@@ -384,8 +392,8 @@
         out_specs=vmem,
         scratch_shapes=[
             V(features.shape, BF16), V(w_in.shape, BF16), V(w_plane.shape, BF16), V(w_depth.shape, BF16),
-            V(w_head.shape, BF16), *[pltpu.SMEM((1,), jnp.int32)] * 3, dma((8,)),
-            V(place.shape, BF16), V(spread.shape, BF16), V(win.shape, F32), V(win_out.shape, F32), dma((4,)),
+            V(w_head.shape, BF16), *[pltpu.SMEM((1,), jnp.int32)] * 3, dma((11,)),
+            V(place.shape, BF16), V(spread.shape, BF16), V(win.shape, F32), V(win_out.shape, F32), dma((8,)),
             V((rows, cin * depth), F32), V((2, 2 * PAD, 6 * PAD), F32), V((2 * rows, 2 * rows), F32), V((3, 2 * rows), F32),
             V((3, 3, rows, plane), BF16), V((2 * rows, plane), BF16), V((2 * rows, plane), BF16),
             V((16, 24, LANES), F32), V((16, 32, LANES), F32),

time: 24.2 us -> 24.3 us (level)
  no operation moved by 1% of the time
where the time goes in v5:
time: 24.3 us; the launch traced here: 24.1 us
  Pallas kernels  20.7 us (85%)
  between operations  1.95 us (8%)
  local copies, waits for them, and re-layouts  1.39 us (6%)
    pallas_call x1, Pallas kernels, on_device(): pl.pallas_call(functools.partial(kernel, n, half), out_shape=jax.ShapeDty...  20.7 us
    unnamed x1, local copies, waits for them, and re-layouts  1.39 us

profile of v5, /device:TPU:0, one launch (start us, length us, event | category | flops | bytes accessed | tf_op | source)
XLA Modules:
  0.0 24.1 jit_solution(10269651739303462843)
XLA Ops:
  1.9 20.7 %shard_map.118 = f32[1,4,2304]{2,1,0:T(4,128)} custom-call(bf16[1,64,4,2304]{3,2,1,0:T(4,128)(2,1)} %feat_h.1, bf16[28,64]{1,0:T(8,128)(2,1)} %w_in_h.1, bf16[9,28,28]{2,1,0:T(8,128)(2,1)} %w_plane_h.1, bf16[3,28,28]{2,1,0:T(8,128)(2,1)} %w_depth_h.1, bf16[3,28]{1,0:T(4,128)(2,1)} %w_head_h.1, s32[1]{0:T(128)S(6)} %copy.14.owner_h, s32[1]{0:T(128)S(6)} %copy.15.anchor_h, ...), custom_call_target="tpu_custom_call" | custom-call | flops 6000000000 | bytes 8000000 | tf_op jit(solution)/shard_map/pallas_call | solution.py:388
  22.7 1.4 %copy.17 = f32[1,4,2304]{2,1,0:T(4,128)} copy(f32[1,4,2304]{2,1,0:T(4,128)} %shard_map.118) | data formatting | bytes 73728

commit v6 on v5

--- a/solution.py
+++ b/solution.py
@@ -11,7 +11,7 @@
 
 MESH = pl.DeviceIdType.MESH
 LANES = 128
-TILE = 256
+TILE = 768
 PAD = 32
 F32 = jnp.float32
 BF16 = jnp.bfloat16

time: 24.3 us -> 24.3 us (level)
  no operation moved by 1% of the time
where the time goes in v6:
time: 24.3 us; the launch traced here: 24.1 us
  Pallas kernels  20.7 us (85%)
  between operations  1.95 us (8%)
  local copies, waits for them, and re-layouts  1.39 us (6%)
    pallas_call x1, Pallas kernels, on_device(): pl.pallas_call(functools.partial(kernel, n, half), out_shape=jax.ShapeDty...  20.7 us
    unnamed x1, local copies, waits for them, and re-layouts  1.39 us

profile of v6, /device:TPU:0, one launch (start us, length us, event | category | flops | bytes accessed | tf_op | source)
XLA Modules:
  0.0 24.1 jit_solution(1493693714110985552)
XLA Ops:
  1.9 20.7 %shard_map.118 = f32[1,4,2304]{2,1,0:T(4,128)} custom-call(bf16[1,64,4,2304]{3,2,1,0:T(4,128)(2,1)} %feat_h.1, bf16[28,64]{1,0:T(8,128)(2,1)} %w_in_h.1, bf16[9,28,28]{2,1,0:T(8,128)(2,1)} %w_plane_h.1, bf16[3,28,28]{2,1,0:T(8,128)(2,1)} %w_depth_h.1, bf16[3,28]{1,0:T(4,128)(2,1)} %w_head_h.1, s32[1]{0:T(128)S(6)} %copy.14.owner_h, s32[1]{0:T(128)S(6)} %copy.15.anchor_h, ...), custom_call_target="tpu_custom_call" | custom-call | flops 6000000000 | bytes 8000000 | tf_op jit(solution)/shard_map/pallas_call | solution.py:388
  22.7 1.4 %copy.17 = f32[1,4,2304]{2,1,0:T(4,128)} copy(f32[1,4,2304]{2,1,0:T(4,128)} %shard_map.118) | data formatting | bytes 73728
